TPU v7x, 128 devices: a whole 4x4x4 slice. The times are simulated.
128 devices in a mesh: pipe: 8 (over x, core), expert: 16 (over z, y).
Axes of the slice: x: 4, y: 4, z: 4, core: 2. Of those that a mesh axis runs over, the one named last changes fastest.
Arguments:
- activations: bfloat16 [1, 2048, 2048], P(None, 'expert'), may hold values from -6 to 6
- norm_gain: bfloat16 [8, 2048], P('pipe'), may hold values from 0.25 to 1.75
- w_gate: bfloat16 [8, 16, 2048, 768], P('pipe', 'expert'), may hold values from -0.125 to 0.125
- w_up: bfloat16 [8, 16, 2048, 768], P('pipe', 'expert'), may hold values from -0.125 to 0.125
- w_down: bfloat16 [8, 16, 768, 2048], P('pipe', 'expert'), may hold values from -0.21875 to 0.21875
- routes: int32 [8, 1, 64, 2], P('pipe', None, 'expert'), may hold values from 0 to 15, as said below
- gate_scores: float32 [8, 1, 64, 2], P('pipe', None, 'expert'), may hold values from 0.25 to 4
Outputs:
- section_out: bfloat16 [8, 1, 2048, 2048], P('pipe', None, 'expert')
Inputs may be any that keep to these rules, and one draw needn't show every extreme that they name: `routes`: each entry names an expert. The 2 experts of one block differ. Among the 4 blocks that one device holds for one section and microbatch, no expert is named more than 1 times; in every section and microbatch one expert is named exactly 1 times by the blocks of every device.
All inputs are finite; a program needn't handle non-finite values.
Results may differ from a plain program's by a relative error of at most 0.024.
Values may be sent and summed in bfloat16 or wider, within the bound.
No kernel may reach another device: no remote copies, remote signals or barrier semaphores. Data moves between devices by JAX's collectives and lax.ppermute only.
A program may use at most 64 MiB of HBM per device.

v0:
```python
import jax
import jax.numpy as jnp
from jax import lax
from jax.experimental import pallas as pl
from jax.experimental.pallas import tpu as pltpu
from jax.sharding import PartitionSpec as P

H_CUT = 256
D_CUT = 512
AHEAD = 3
STREAMED = (0,)
K_CUT = 512
DOWN_PARTS = 3
SMALL = pltpu.CompilerParams(vmem_limit_bytes=8 * 1024 * 1024)


def in_vmem(x):
    return pltpu.with_memory_space_constraint(x, pltpu.VMEM)


def in_hbm(x):
    return pltpu.with_memory_space_constraint(x, pltpu.HBM)


def spec(space):
    return pl.BlockSpec(memory_space=space)


def core_of(section_ref):
    return section_ref[0] & 1


def normalised(hidden, gain_row):
    scaled = lax.rsqrt(jnp.mean(hidden * hidden, axis=-1, keepdims=True) + 1e-06)
    return (hidden * scaled * gain_row).astype(jnp.bfloat16)


def mixed(which, ids_ref, scores_ref, hidden_ref, returned_ref, block):
    topk = ids_ref.shape[1]
    parts = [scores_ref[which, k, block] for k in range(topk)]
    whole = parts[0]
    for k in range(1, topk):
        whole = whole + parts[k]
    total = None
    for k in range(topk):
        weight = jnp.full((1, 1), parts[k], jnp.float32) / jnp.full((1, 1), whole, jnp.float32)
        term = returned_ref[ids_ref[which, k, block]].astype(jnp.float32) * weight
        total = term if total is None else total + term
    return (hidden_ref[block].astype(jnp.float32) + total).astype(jnp.bfloat16)


def pack(ids, normed_ref, packed_ref):
    for expert in range(packed_ref.shape[0]):
        block = jnp.int32(0)
        for b in range(1, len(ids)):
            for one in ids[b]:
                block = jnp.where(one == expert, jnp.int32(b), block)
        packed_ref[expert] = normed_ref[block]


def table_ids(which, ids_ref):
    topk, blocks = ids_ref.shape[1:]
    return [[ids_ref[which, k, b] for k in range(topk)] for b in range(blocks)]


def first_kernel(
    section_ref, rx_h, sx_h, gx, ro_h, so_h, go, x_hbm, gate, up, down,
    hidden_ref, packed_ref, gains_ref, gate_v, up_v, down_v, ids_ref, scores_ref,
    ro, rx, so, sx, normed_ref, gain_v, sems, weight_sems,
):
    core = core_of(section_ref)
    first = core == 0
    pairs = (
        (ro_h, ro), (rx_h, rx), (so_h, so), (sx_h, sx),
        (go, gain_v.at[0]), (gx, gain_v.at[1]), (x_hbm.at[:, core], hidden_ref),
    )
    copies = [pltpu.make_async_copy(source, target, sems.at[i]) for i, (source, target) in enumerate(pairs)]
    for copy in copies:
        copy.start()
    for copy in copies:
        copy.wait()
    loads = [
        pltpu.make_async_copy(source, target, weight_sems.at[i])
        for i, (source, target) in enumerate(((gate, gate_v), (up, up_v), (down, down_v)))
    ]

    topk, blocks = ro.shape
    ids = [[None] * topk for _ in range(blocks)]
    for b in range(blocks):
        for k in range(topk):
            ids[b][k] = jnp.where(first, ro[k, b], rx[k, b])
            ids_ref[0, k, b] = ids[b][k]
            ids_ref[1, k, b] = jnp.where(first, rx[k, b], ro[k, b])
            scores_ref[0, k, b] = jnp.where(first, so[k, b], sx[k, b])
            scores_ref[1, k, b] = jnp.where(first, sx[k, b], so[k, b])
    own = gain_v[0].astype(jnp.float32)
    other = gain_v[1].astype(jnp.float32)
    gain = jnp.where(first, own, other)
    gains_ref[0] = gain
    gains_ref[1] = jnp.where(first, other, own)
    for block in range(hidden_ref.shape[0]):
        normed_ref[block] = normalised(hidden_ref[block].astype(jnp.float32), gain)
    pack(ids, normed_ref, packed_ref)

    @pl.when(first)
    def _():
        for copy in loads:
            copy.start()
        for copy in loads:
            copy.wait()


def first_call(held, slots, section_table, route, route_x, score, score_x, whole_x, gain, gain_x, own):
    width = held[2]
    both = (2,) + route.shape
    return pl.pallas_call(
        first_kernel,
        out_shape=(
            pltpu.VMEM(held, jnp.bfloat16),
            pltpu.VMEM(slots, jnp.bfloat16),
            pltpu.VMEM((2, 1, width), jnp.float32),
            *[pltpu.VMEM(w.shape, w.dtype) for w in own],
            pltpu.SMEM(both, jnp.int32),
            pltpu.SMEM(both, jnp.float32),
        ),
        in_specs=[spec(pltpu.SMEM)] + [spec(pl.ANY)] * 3 + [spec(pltpu.HBM)] * 7,
        out_specs=(spec(pltpu.VMEM),) * 6 + (spec(pltpu.SMEM),) * 2,
        scratch_shapes=[
            pltpu.SMEM(route.shape, jnp.int32),
            pltpu.SMEM(route.shape, jnp.int32),
            pltpu.SMEM(route.shape, jnp.float32),
            pltpu.SMEM(route.shape, jnp.float32),
            pltpu.VMEM(held, jnp.bfloat16),
            pltpu.VMEM((2, 1, width), jnp.bfloat16),
            pltpu.SemaphoreType.DMA((7,)),
            pltpu.SemaphoreType.DMA((3,)),
        ],
        compiler_params=SMALL,
        name="slice_norm_pack",
    )(section_table, route_x, score_x, gain_x, *[in_hbm(v) for v in (route, score, gain, whole_x, *own)])


def enter_kernel(ids_ref, hidden_ref, gains_ref, packed_ref, normed_ref):
    for block in range(hidden_ref.shape[0]):
        normed_ref[block] = normalised(hidden_ref[block].astype(jnp.float32), gains_ref[0])
    pack(table_ids(0, ids_ref), normed_ref, packed_ref)


def between_kernel(ids_ref, scores_ref, hidden_ref, returned_ref, gains_ref, out_ref, packed_ref, normed_ref):
    for block in range(hidden_ref.shape[0]):
        result = mixed(0, ids_ref, scores_ref, hidden_ref, returned_ref, block)
        out_ref[block] = result
        normed_ref[block] = normalised(result.astype(jnp.float32), gains_ref[1])
    pack(table_ids(1, ids_ref), normed_ref, packed_ref)


def leave_kernel(ids_ref, scores_ref, hidden_ref, returned_ref, out_ref):
    for block in range(hidden_ref.shape[0]):
        out_ref[block] = mixed(1, ids_ref, scores_ref, hidden_ref, returned_ref, block)


def finish_kernel(section_ref, ids_ref, scores_ref, hidden_ref, returned_ref, *refs):
    earlier, (kept_ref, sent_ref, last_ref, sems) = refs[:-4], refs[-4:]
    stages = (len(earlier) + 1) // 2
    for block in range(hidden_ref.shape[0]):
        last_ref[block] = mixed(1, ids_ref, scores_ref, hidden_ref, returned_ref, block)
    results_a, results_b = earlier[:stages], (*earlier[stages:], last_ref)
    for step in range(stages):
        for core, targets in ((0, (kept_ref, sent_ref)), (1, (sent_ref, kept_ref))):

            @pl.when(section_ref[0] == 2 * step + core)
            def _():
                for i, source in enumerate((results_a[step], results_b[step])):
                    pltpu.make_async_copy(source, targets[i], sems.at[i]).start()

    for i, target in enumerate((kept_ref, sent_ref)):
        pltpu.make_async_copy(results_a[0], target, sems.at[i]).wait()


def finish(section_table, ids, scores, hidden, returned, earlier):
    held = hidden.shape
    return pl.pallas_call(
        finish_kernel,
        out_shape=(pltpu.VMEM(held, jnp.bfloat16),) * 2,
        in_specs=[spec(pltpu.SMEM)] * 3 + [spec(pltpu.VMEM)] * 2 + [spec(pl.ANY)] * len(earlier),
        out_specs=(spec(pltpu.VMEM),) * 2,
        scratch_shapes=[pltpu.VMEM(held, jnp.bfloat16), pltpu.SemaphoreType.DMA((2,))],
        compiler_params=SMALL,
        name="mix_choose",
    )(section_table, ids, scores, in_vmem(hidden), in_vmem(returned), *earlier)


def join_kernel(section_ref, kept_ref, got_ref, out_ref, sems):
    copies = [
        pltpu.make_async_copy(kept_ref, out_ref.at[:, core_of(section_ref)], sems.at[0]),
        pltpu.make_async_copy(got_ref, out_ref.at[:, 1 - core_of(section_ref)], sems.at[1]),
    ]
    for copy in copies:
        copy.start()
    for copy in copies:
        copy.wait()


def join(section_table, kept, got):
    blocks, lane, width = kept.shape
    return pl.pallas_call(
        join_kernel,
        out_shape=pltpu.HBM((blocks, 2, lane, width), jnp.bfloat16),
        in_specs=[spec(pltpu.SMEM)] + [spec(pltpu.VMEM)] * 2,
        out_specs=spec(pltpu.HBM),
        scratch_shapes=[pltpu.SemaphoreType.DMA((2,))],
        compiler_params=SMALL,
        name="join_rows",
    )(section_table, in_vmem(kept), in_vmem(got))


def small_call(kernel, name, outs, scratch, smem, vmem):
    single = len(outs) == 1
    shapes = tuple(pltpu.VMEM(o, jnp.bfloat16) for o in outs)
    specs = tuple(spec(pltpu.VMEM) for _ in outs)
    return pl.pallas_call(
        kernel,
        out_shape=shapes[0] if single else shapes,
        in_specs=[spec(pltpu.SMEM)] * len(smem) + [spec(pltpu.VMEM)] * len(vmem),
        out_specs=specs[0] if single else specs,
        scratch_shapes=[pltpu.VMEM(s, jnp.bfloat16) for s in scratch],
        compiler_params=SMALL,
        name=name,
    )(*smem, *[in_vmem(v) for v in vmem])


def silu_times(gate_part, up_part):
    return (gate_part / (1.0 + jnp.exp(-gate_part)) * up_part).astype(jnp.bfloat16)


def down_part(active_v, down_ref, out_ref):
    for c in range(down_ref.shape[1] // D_CUT):
        cut = pl.ds(c * D_CUT, D_CUT)
        produced = jnp.dot(active_v[...], down_ref[:, cut], preferred_element_type=jnp.float32)
        out_ref[:, cut] = produced.astype(jnp.bfloat16)


def load_copies(sources, targets, sems):
    (gate, up, down), (gate_ref, up_ref, down_ref) = sources, targets
    parts = gate_ref.shape[0] // K_CUT
    down_rows = down_ref.shape[0] // DOWN_PARTS
    made = []
    for c in range(parts):
        cut = pl.ds(c * K_CUT, K_CUT)
        made.append(pltpu.make_async_copy(gate.at[cut], gate_ref.at[cut], sems.at[2 * c]))
        made.append(pltpu.make_async_copy(up.at[cut], up_ref.at[cut], sems.at[2 * c + 1]))
    for c in range(DOWN_PARTS):
        cut = pl.ds(c * down_rows, down_rows)
        made.append(pltpu.make_async_copy(down.at[cut], down_ref.at[cut], sems.at[2 * parts + c]))
    return made


def streamed_ffn(x_ref, targets, out_ref, active_v, gate_sum, up_sum, down_sum, ready):
    gate_ref, up_ref, down_ref = targets
    parts = gate_ref.shape[0] // K_CUT
    for c in range(parts):
        cut = pl.ds(c * K_CUT, K_CUT)
        for i, weight_ref, sum_ref in ((2 * c, gate_ref, gate_sum), (2 * c + 1, up_ref, up_sum)):
            ready(i)
            term = jnp.dot(x_ref[:, cut], weight_ref[cut, :], preferred_element_type=jnp.float32)
            sum_ref[...] = term if c == 0 else sum_ref[...] + term
    active_v[...] = silu_times(gate_sum[...], up_sum[...])
    down_rows = down_ref.shape[0] // DOWN_PARTS
    for c in range(DOWN_PARTS):
        ready(2 * parts + c)
        cut = pl.ds(c * down_rows, down_rows)
        term = jnp.dot(active_v[:, cut], down_ref[cut, :], preferred_element_type=jnp.float32)
        if c == 0:
            down_sum[...] = term
        elif c < DOWN_PARTS - 1:
            down_sum[...] += term
        else:
            out_ref[...] = (down_sum[...] + term).astype(jnp.bfloat16)


def stream_on_core_1(section_ref, copies):
    def start():
        @pl.when(core_of(section_ref) != 0)
        def _():
            for copy in copies:
                copy.start()

    def ready(i):
        @pl.when(core_of(section_ref) != 0)
        def _():
            copies[i].wait()

    return start, ready


def first_ffn_kernel(
    section_ref, x_ref, gi, ui, di, gx, ux, dx, out_ref, gate_ref, up_ref, down_ref, gate_next, up_next, down_next,
    active_v, gate_sum, up_sum, down_sum, sems
):
    targets = (gate_ref, up_ref, down_ref)
    start, ready = stream_on_core_1(section_ref, load_copies((gx, ux, dx), targets, sems))
    copies = load_copies((gx, ux, dx), (gate_next, up_next, down_next), sems)
    start()

    @pl.when(core_of(section_ref) == 0)
    def _():
        for copy in copies:
            copy.start()
        for copy in copies[:AHEAD]:
            copy.wait()

    streamed_ffn(x_ref, targets, out_ref, active_v, gate_sum, up_sum, down_sum, ready)

    @pl.when(core_of(section_ref) == 0)
    def _():
        for copy in copies[AHEAD:]:
            copy.wait()


def second_ffn_kernel(
    section_ref, x_ref, gi, ui, di, g_h, u_h, d_h, out_ref, gate_ref, up_ref, down_ref,
    active_v, gate_sum, up_sum, down_sum, sems
):
    targets = (gate_ref, up_ref, down_ref)
    start, ready = stream_on_core_1(section_ref, load_copies((g_h, u_h, d_h), targets, sems))
    start()
    streamed_ffn(x_ref, targets, out_ref, active_v, gate_sum, up_sum, down_sum, ready)


def later_ffn_kernel(
    section_ref, x_ref, gi, ui, di, g_h, u_h, d_h, out_ref, gate_ref, up_ref, down_ref,
    active_v, gate_sum, up_sum, down_sum, sems
):
    @pl.when(core_of(section_ref) != 0)
    def _():
        copies = load_copies((g_h, u_h, d_h), (gate_ref, up_ref, down_ref), sems)
        for copy in copies:
            copy.start()
        for copy in copies:
            copy.wait()

    ffn_kernel(x_ref, gate_ref, up_ref, down_ref, out_ref, active_v)


def ffn_cost(flat, hidden):
    rows, width = flat.shape
    return pl.CostEstimate(
        flops=6 * rows * width * hidden,
        bytes_accessed=6 * width * hidden + 4 * rows * width,
        transcendentals=rows * hidden,
    )


def load_ffn(kernel, section_table, received, present, sources, anywhere, extra=0):
    experts, rows, width = received.shape
    hidden = present[0].shape[1]
    flat = received.reshape(experts * rows, width)
    sums = pltpu.VMEM((flat.shape[0], hidden), jnp.float32)
    produced, *weights = pl.pallas_call(
        kernel,
        out_shape=(
            pltpu.VMEM(flat.shape, jnp.bfloat16),
            *[pltpu.VMEM(w.shape, w.dtype) for w in present] * (1 + extra),
        ),
        in_specs=[spec(pltpu.SMEM)] + [spec(pltpu.VMEM)] * 4 + [spec(pl.ANY if anywhere else pltpu.HBM)] * 3,
        out_specs=(spec(pltpu.VMEM),) * (4 + 3 * extra),
        scratch_shapes=[
            pltpu.VMEM((flat.shape[0], hidden), jnp.bfloat16),
            sums,
            sums,
            pltpu.VMEM(flat.shape, jnp.float32),
            pltpu.SemaphoreType.DMA((2 * (width // K_CUT) + DOWN_PARTS,)),
        ],
        input_output_aliases={2: 1, 3: 2, 4: 3},
        compiler_params=SMALL,
        cost_estimate=ffn_cost(flat, hidden),
        name="load_expert_ffn",
    )(
        section_table,
        in_vmem(flat),
        *[in_vmem(w) for w in present],
        *(sources if anywhere else [in_hbm(w) for w in sources]),
    )
    return produced.reshape(received.shape), weights


def ffn_kernel(x_ref, gate_ref, up_ref, down_ref, out_ref, active_v):
    for c in range(gate_ref.shape[1] // H_CUT):
        cut = pl.ds(c * H_CUT, H_CUT)
        gate_part = jnp.dot(x_ref[...], gate_ref[:, cut], preferred_element_type=jnp.float32)
        up_part = jnp.dot(x_ref[...], up_ref[:, cut], preferred_element_type=jnp.float32)
        active_v[:, cut] = silu_times(gate_part, up_part)
    down_part(active_v, down_ref, out_ref)


def exchange(slots):
    return lax.all_to_all(slots, "expert", 0, 0, tiled=True)


def relay_pairs(step, stages):
    place = list(range(stages))
    for x in range(step % 2, stages - 1, 2):
        place[x], place[x + 1] = x + 1, x
    return [(2 * x + c, 2 * place[x] + c) for x in range(stages) for c in range(2)]


def shards(activations, norm_gain, w_gate, w_up, w_down, routes, gate_scores):
    sections = lax.axis_size("pipe")
    experts = lax.axis_size("expert")
    section = lax.axis_index("pipe")
    stages = sections // 2
    blocks, topk = routes.shape[2:]
    rows = activations.shape[1] // blocks
    lane = rows // 2
    width = activations.shape[2]
    held = (blocks, lane, width)
    slots = (experts, lane, width)
    swap = [(i, i ^ 1) for i in range(sections)]

    def swapped(x):
        return lax.ppermute(x, "pipe", swap)

    route = routes[0, 0].T
    score = gate_scores[0, 0].T
    route_x, gain_x, score_x = swapped(route), swapped(norm_gain), swapped(score)
    own = (w_gate[0, 0], w_up[0, 0], w_down[0, 0])
    *own, route_x, gain_x, score_x = lax.optimization_barrier((*own, route_x, gain_x, score_x))
    other = tuple(swapped(w) for w in own)
    section_table = section.astype(jnp.int32).reshape(1)

    whole_x = activations[0].reshape(blocks, 2, lane, width)
    hidden, sent, gains, *weights_a, ids, scores = first_call(
        held, slots, section_table, route, route_x, score, score_x, whole_x, norm_gain, gain_x, own
    )
    out_a, out_b = [], []
    for step in range(stages):
        received = exchange(sent)
        if step == 0:
            made, weights = load_ffn(first_ffn_kernel, section_table, received, weights_a, other, True, 1)
            weights_a, weights_b = weights[:3], weights[3:]
        else:
            made, weights_a = load_ffn(later_ffn_kernel, section_table, received, weights_a, other, True)
        hidden, sent = small_call(
            between_kernel, "mix_norm_pack", (held, slots), (held,), (ids, scores), (hidden, exchange(made), gains)
        )
        out_a.append(hidden)
        received = exchange(sent)
        kernel = second_ffn_kernel if step in STREAMED else later_ffn_kernel
        made, weights_b = load_ffn(kernel, section_table, received, weights_b, own, False)
        back = exchange(made)
        if step == stages - 1:
            break
        hidden = small_call(leave_kernel, "mix", (held,), (), (ids, scores), (hidden, back))
        out_b.append(hidden)
        hidden = lax.ppermute(hidden, "pipe", relay_pairs(step, stages))
        sent = small_call(enter_kernel, "norm_pack", (slots,), (held,), (ids,), (hidden, gains))

    kept, leaving = finish(section_table, ids, scores, hidden, back, out_a + out_b)
    whole = join(section_table, kept, swapped(leaving))
    return whole.reshape(1, 1, blocks * rows, width)


def solution(mesh):
    in_specs = (
        P(None, "expert", None),
        P("pipe", None),
        P("pipe", "expert", None, None),
        P("pipe", "expert", None, None),
        P("pipe", "expert", None, None),
        P("pipe", None, "expert", None),
        P("pipe", None, "expert", None),
    )
    out_specs = P("pipe", None, "expert", None)
    return jax.shard_map(shards, mesh=mesh, in_specs=in_specs, out_specs=out_specs, check_vma=False)
```

profile of v0, /device:TPU:1, one launch (start us, length us, event | category | flops | bytes accessed | tf_op | source)
XLA Modules:
  0.0 320.7 jit_solution(7551112056973936793)
XLA Ops:
  0.0 1.4 collective-permute-start.1
  1.4 0.5 collective-permute-start.2
  1.9 0.8 collective-permute-done.rx_h
  2.8 0.2 collective-permute-done.2.sx_h
  3.0 0.3 collective-permute-start.3
  3.3 0.2 collective-permute-start.4
  3.5 0.3 collective-permute-start.5
  3.8 1.3 slice_norm_pack.1
  5.1 20.8 %all_to_all.80 = bf16[16,16,2048]{2,1,0:T(8,128)(2,1)S(1)} all-to-all(bf16[16,16,2048]{2,1,0:T(8,128)(2,1)S(1)} %get-tuple-element.67), channel_id=1, replica_groups=mesh['pipe'=8,'expert'=16] {'expert'}, dimensions={0} | all-to-all | bytes 2097152 | tf_op jit(solution)/shard_map/all_to_all | solution.py:397
  25.9 4.8 %load_expert_ffn.8 = (bf16[256,2048]{1,0:T(8,128)(2,1)S(1)}, bf16[2048,768]{1,0:T(8,128)(2,1)S(1)}, bf16[2048,768]{1,0:T(8,128)(2,1)S(1)}, bf16[768,2048]{1,0:T(...) custom-call(s32[1]{0:T(128)} %bitcast.section_ref, ...), custom_call_target="tpu_custom_call", output_to_operand_aliasing={{1}: (2, {}), {2}: (3, {}), {3}: (4, {})} | custom-call | flops 2415919104 | bytes 11534336 | tf_op jit(solution)/shard_map/load_expert_ffn/pallas_call | solution.py:359
  30.7 15.1 %all_to_all.81.returned_ref = bf16[16,16,2048]{2,1,0:T(8,128)(2,1)S(1)} all-to-all(bf16[16,16,2048]{2,1,0:T(8,128)(2,1)S(1)} %bitcast.36), channel_id=1, replica_groups=mesh['pipe'=8,'expert'=16] {'expert'}, dimensions={0} | all-to-all | bytes 2097152 | tf_op jit(solution)/shard_map/all_to_all | solution.py:397
  45.8 0.4 mix_norm_pack.4
  46.2 14.6 %all_to_all.82 = bf16[16,16,2048]{2,1,0:T(8,128)(2,1)S(1)} all-to-all(bf16[16,16,2048]{2,1,0:T(8,128)(2,1)S(1)} %get-tuple-element.74), channel_id=1, replica_groups=mesh['pipe'=8,'expert'=16] {'expert'}, dimensions={0} | all-to-all | bytes 2097152 | tf_op jit(solution)/shard_map/all_to_all | solution.py:397
  60.8 5.1 %load_expert_ffn.9 = (bf16[256,2048]{1,0:T(8,128)(2,1)S(1)}, bf16[2048,768]{1,0:T(8,128)(2,1)S(1)}, bf16[2048,768]{1,0:T(8,128)(2,1)S(1)}, bf16[768,2048]{1,0:T(8,128)(2,1)S(1)}) custom-call(s32[1]{0:T(128)} %bitcast.section_ref, bf16[256,2048]{1,0:T(8,128)(2,1)S(1)} %bitcast.35, ...), custom_call_target="tpu_custom_call", output_to_operand_aliasing={{1}: (2, {}), {2}: (3, {}), {3}: (4, {})} | custom-call | flops 2415919104 | bytes 11534336 | tf_op jit(solution)/shard_map/load_expert_ffn/pallas_call | solution.py:359
  65.9 14.8 %all_to_all.83.returned_ref = bf16[16,16,2048]{2,1,0:T(8,128)(2,1)S(1)} all-to-all(bf16[16,16,2048]{2,1,0:T(8,128)(2,1)S(1)} %bitcast.38), channel_id=1, replica_groups=mesh['pipe'=8,'expert'=16] {'expert'}, dimensions={0} | all-to-all | bytes 2097152 | tf_op jit(solution)/shard_map/all_to_all | solution.py:397
  80.8 1.3 collective-permute-start.6
  82.1 4.3 %collective-permute-done.6.hidden_ref = bf16[4,16,2048]{2,1,0:T(8,128)(2,1)S(1)} collective-permute-done((bf16[4,16,2048]{2,1,0:T(8,128)(2,1)S(1)}, bf16[4,16,2048]{2,1,0:T(8,128)(2,1)S(1)}, u32[]{:S(2)}, u32[]{:S(2)}) %collective-permute-start.6) | collective-permute-done | bytes 262176 | tf_op jit(solution)/shard_map/ppermute | solution.py:455
  86.4 0.2 norm_pack.3
  86.7 14.5 %all_to_all.84 = bf16[16,16,2048]{2,1,0:T(8,128)(2,1)S(1)} all-to-all(bf16[16,16,2048]{2,1,0:T(8,128)(2,1)S(1)} %norm_pack.3), channel_id=1, replica_groups=mesh['pipe'=8,'expert'=16] {'expert'}, dimensions={0} | all-to-all | bytes 2097152 | tf_op jit(solution)/shard_map/all_to_all | solution.py:397
  101.1 5.6 %load_expert_ffn.10 = (bf16[256,2048]{1,0:T(8,128)(2,1)S(1)}, bf16[2048,768]{1,0:T(8,128)(2,1)S(1)}, bf16[2048,768]{1,0:T(8,128)(2,1)S(1)}, bf16[768,2048]{1,0:T(8,128)(2,1)S(1)}) custom-call(s32[1]{0:T(128)} %bitcast.section_ref, bf16[256,2048]{1,0:T(8,128)(2,1)S(1)} %bitcast.30, ...), custom_call_target="tpu_custom_call", output_to_operand_aliasing={{1}: (2, {}), {2}: (3, {}), {3}: (4, {})} | custom-call | flops 2415919104 | bytes 11534336 | tf_op jit(solution)/shard_map/load_expert_ffn/pallas_call | solution.py:359
  106.7 14.7 %all_to_all.85.returned_ref = bf16[16,16,2048]{2,1,0:T(8,128)(2,1)S(1)} all-to-all(bf16[16,16,2048]{2,1,0:T(8,128)(2,1)S(1)} %bitcast.39), channel_id=1, replica_groups=mesh['pipe'=8,'expert'=16] {'expert'}, dimensions={0} | all-to-all | bytes 2097152 | tf_op jit(solution)/shard_map/all_to_all | solution.py:397
  121.5 0.4 mix_norm_pack.5
  121.8 14.5 %all_to_all.86 = bf16[16,16,2048]{2,1,0:T(8,128)(2,1)S(1)} all-to-all(bf16[16,16,2048]{2,1,0:T(8,128)(2,1)S(1)} %get-tuple-element.84), channel_id=1, replica_groups=mesh['pipe'=8,'expert'=16] {'expert'}, dimensions={0} | all-to-all | bytes 2097152 | tf_op jit(solution)/shard_map/all_to_all | solution.py:397
  136.3 6.4 %load_expert_ffn.11 = (bf16[256,2048]{1,0:T(8,128)(2,1)S(1)}, bf16[2048,768]{1,0:T(8,128)(2,1)S(1)}, bf16[2048,768]{1,0:T(8,128)(2,1)S(1)}, bf16[768,2048]{1,0:T(8,128)(2,1)S(1)}) custom-call(s32[1]{0:T(128)} %bitcast.section_ref, bf16[256,2048]{1,0:T(8,128)(2,1)S(1)} %bitcast.31, ...), custom_call_target="tpu_custom_call", output_to_operand_aliasing={{1}: (2, {}), {2}: (3, {}), {3}: (4, {})} | custom-call | flops 2415919104 | bytes 11534336 | tf_op jit(solution)/shard_map/load_expert_ffn/pallas_call | solution.py:359
  142.7 14.6 %all_to_all.87.returned_ref = bf16[16,16,2048]{2,1,0:T(8,128)(2,1)S(1)} all-to-all(bf16[16,16,2048]{2,1,0:T(8,128)(2,1)S(1)} %bitcast.40), channel_id=1, replica_groups=mesh['pipe'=8,'expert'=16] {'expert'}, dimensions={0} | all-to-all | bytes 2097152 | tf_op jit(solution)/shard_map/all_to_all | solution.py:397
  157.5 0.7 collective-permute-start.7
  158.2 0.2 norm_pack.4
  158.4 14.5 %all_to_all.88 = bf16[16,16,2048]{2,1,0:T(8,128)(2,1)S(1)} all-to-all(bf16[16,16,2048]{2,1,0:T(8,128)(2,1)S(1)} %norm_pack.4), channel_id=1, replica_groups=mesh['pipe'=8,'expert'=16] {'expert'}, dimensions={0} | all-to-all | bytes 2097152 | tf_op jit(solution)/shard_map/all_to_all | solution.py:397
  172.9 5.6 %load_expert_ffn.12 = (bf16[256,2048]{1,0:T(8,128)(2,1)S(1)}, bf16[2048,768]{1,0:T(8,128)(2,1)S(1)}, bf16[2048,768]{1,0:T(8,128)(2,1)S(1)}, bf16[768,2048]{1,0:T(8,128)(2,1)S(1)}) custom-call(s32[1]{0:T(128)} %bitcast.section_ref, bf16[256,2048]{1,0:T(8,128)(2,1)S(1)} %bitcast.32, ...), custom_call_target="tpu_custom_call", output_to_operand_aliasing={{1}: (2, {}), {2}: (3, {}), {3}: (4, {})} | custom-call | flops 2415919104 | bytes 11534336 | tf_op jit(solution)/shard_map/load_expert_ffn/pallas_call | solution.py:359
  178.5 14.6 %all_to_all.89.returned_ref = bf16[16,16,2048]{2,1,0:T(8,128)(2,1)S(1)} all-to-all(bf16[16,16,2048]{2,1,0:T(8,128)(2,1)S(1)} %bitcast.41), channel_id=1, replica_groups=mesh['pipe'=8,'expert'=16] {'expert'}, dimensions={0} | all-to-all | bytes 2097152 | tf_op jit(solution)/shard_map/all_to_all | solution.py:397
  193.1 0.4 mix_norm_pack.6
  193.5 14.5 %all_to_all.90 = bf16[16,16,2048]{2,1,0:T(8,128)(2,1)S(1)} all-to-all(bf16[16,16,2048]{2,1,0:T(8,128)(2,1)S(1)} %get-tuple-element.94), channel_id=1, replica_groups=mesh['pipe'=8,'expert'=16] {'expert'}, dimensions={0} | all-to-all | bytes 2097152 | tf_op jit(solution)/shard_map/all_to_all | solution.py:397
  208.0 6.4 %load_expert_ffn.13 = (bf16[256,2048]{1,0:T(8,128)(2,1)S(1)}, bf16[2048,768]{1,0:T(8,128)(2,1)S(1)}, bf16[2048,768]{1,0:T(8,128)(2,1)S(1)}, bf16[768,2048]{1,0:T(8,128)(2,1)S(1)}) custom-call(s32[1]{0:T(128)} %bitcast.section_ref, bf16[256,2048]{1,0:T(8,128)(2,1)S(1)} %bitcast.33, ...), custom_call_target="tpu_custom_call", output_to_operand_aliasing={{1}: (2, {}), {2}: (3, {}), {3}: (4, {})} | custom-call | flops 2415919104 | bytes 11534336 | tf_op jit(solution)/shard_map/load_expert_ffn/pallas_call | solution.py:359
  214.4 15.2 %all_to_all.91.returned_ref = bf16[16,16,2048]{2,1,0:T(8,128)(2,1)S(1)} all-to-all(bf16[16,16,2048]{2,1,0:T(8,128)(2,1)S(1)} %bitcast.42), channel_id=1, replica_groups=mesh['pipe'=8,'expert'=16] {'expert'}, dimensions={0} | all-to-all | bytes 2097152 | tf_op jit(solution)/shard_map/all_to_all | solution.py:397
  229.8 6.9 %collective-permute-start.8 = (bf16[4,16,2048]{2,1,0:T(8,128)(2,1)S(1)}, bf16[4,16,2048]{2,1,0:T(8,128)(2,1)S(1)}, u32[]{:S(2)}, u32[]{:S(2)}) collective-permute-start(bf16[4,16,2048]{2,1,0:T(8,128)(2,1)S(1)} %mix.5.refs_6_), channel_id=1, source_target_pairs={{0,32},{16,48},{32,0},{48,16},{64,96},{80,112},{96,64},{112,80},{1... | collective-permute-start | bytes 786440 | tf_op jit(solution)/shard_map/ppermute | solution.py:455
  236.7 3.8 %collective-permute-done.8.hidden_ref = bf16[4,16,2048]{2,1,0:T(8,128)(2,1)S(1)} collective-permute-done((bf16[4,16,2048]{2,1,0:T(8,128)(2,1)S(1)}, bf16[4,16,2048]{2,1,0:T(8,128)(2,1)S(1)}, u32[]{:S(2)}, u32[]{:S(2)}) %collective-permute-start.8) | collective-permute-done | bytes 262176 | tf_op jit(solution)/shard_map/ppermute | solution.py:455
  240.5 0.2 norm_pack.5
  240.7 14.5 %all_to_all.92 = bf16[16,16,2048]{2,1,0:T(8,128)(2,1)S(1)} all-to-all(bf16[16,16,2048]{2,1,0:T(8,128)(2,1)S(1)} %norm_pack.5), channel_id=1, replica_groups=mesh['pipe'=8,'expert'=16] {'expert'}, dimensions={0} | all-to-all | bytes 2097152 | tf_op jit(solution)/shard_map/all_to_all | solution.py:397
  255.2 5.6 %load_expert_ffn.14 = (bf16[256,2048]{1,0:T(8,128)(2,1)S(1)}, bf16[2048,768]{1,0:T(8,128)(2,1)S(1)}, bf16[2048,768]{1,0:T(8,128)(2,1)S(1)}, bf16[768,2048]{1,0:T(8,128)(2,1)S(1)}) custom-call(s32[1]{0:T(128)} %bitcast.section_ref, bf16[256,2048]{1,0:T(8,128)(2,1)S(1)} %bitcast.29, ...), custom_call_target="tpu_custom_call", output_to_operand_aliasing={{1}: (2, {}), {2}: (3, {}), {3}: (4, {})} | custom-call | flops 2415919104 | bytes 11534336 | tf_op jit(solution)/shard_map/load_expert_ffn/pallas_call | solution.py:359
  260.8 14.6 %all_to_all.93.returned_ref = bf16[16,16,2048]{2,1,0:T(8,128)(2,1)S(1)} all-to-all(bf16[16,16,2048]{2,1,0:T(8,128)(2,1)S(1)} %bitcast.37), channel_id=1, replica_groups=mesh['pipe'=8,'expert'=16] {'expert'}, dimensions={0} | all-to-all | bytes 2097152 | tf_op jit(solution)/shard_map/all_to_all | solution.py:397
  275.4 0.4 mix_norm_pack.7
  275.8 14.5 %all_to_all.94 = bf16[16,16,2048]{2,1,0:T(8,128)(2,1)S(1)} all-to-all(bf16[16,16,2048]{2,1,0:T(8,128)(2,1)S(1)} %get-tuple-element.104), channel_id=1, replica_groups=mesh['pipe'=8,'expert'=16] {'expert'}, dimensions={0} | all-to-all | bytes 2097152 | tf_op jit(solution)/shard_map/all_to_all | solution.py:397
  290.3 6.4 %load_expert_ffn.15 = (bf16[256,2048]{1,0:T(8,128)(2,1)S(1)}, bf16[2048,768]{1,0:T(8,128)(2,1)S(1)}, bf16[2048,768]{1,0:T(8,128)(2,1)S(1)}, bf16[768,2048]{1,0:T(8,128)(2,1)S(1)}) custom-call(s32[1]{0:T(128)} %bitcast.section_ref, bf16[256,2048]{1,0:T(8,128)(2,1)S(1)} %bitcast.34, ...), custom_call_target="tpu_custom_call", output_to_operand_aliasing={{1}: (2, {}), {2}: (3, {}), {3}: (4, {})} | custom-call | flops 2415919104 | bytes 11534336 | tf_op jit(solution)/shard_map/load_expert_ffn/pallas_call | solution.py:359
  296.7 14.6 %all_to_all.95.returned_ref = bf16[16,16,2048]{2,1,0:T(8,128)(2,1)S(1)} all-to-all(bf16[16,16,2048]{2,1,0:T(8,128)(2,1)S(1)} %bitcast.43), channel_id=1, replica_groups=mesh['pipe'=8,'expert'=16] {'expert'}, dimensions={0} | all-to-all | bytes 2097152 | tf_op jit(solution)/shard_map/all_to_all | solution.py:397
  311.3 0.3 mix_choose.1
  311.5 7.0 %collective-permute-start.9 = (bf16[4,16,2048]{2,1,0:T(8,128)(2,1)S(1)}, bf16[4,16,2048]{2,1,0:T(8,128)(2,1)S(1)}, u32[]{:S(2)}, u32[]{:S(2)}) collective-permute-start(bf16[4,16,2048]{2,1,0:T(8,128)(2,1)S(1)} %get-tuple-element.110), channel_id=1, source_target_pairs={{0,16},{16,0},{32,48},{48,32},{64,80},{80,64},{96,112},{112,96},{1... | collective-permute-start | bytes 786440 | tf_op jit(solution)/shard_map/ppermute | solution.py:421
  318.5 1.2 collective-permute-done.9.got_ref
  319.7 0.8 join_rows.1
  (9 shorter events, 0.5 us)
Async XLA Ops:
  0.0 3.0 collective-permute-start.1
  1.4 1.4 collective-permute-start
  1.4 1.5 collective-permute-start.2
  3.0 22.9 %collective-permute-start.3 = (bf16[2048,768]{1,0:T(8,128)(2,1)}, bf16[2048,768]{1,0:T(8,128)(2,1)S(1)}, u32[]{:S(2)}, u32[]{:S(2)}) collective-permute-start(bf16[2048,768]{1,0:T(8,128)(2,1)} %bitcast.44), channel_id=1, source_target_pairs={{0,16},{16,0},{32,48},{48,32},{64,80},{80,64},{96,112},{112,96},{1... | collective-permute-start | bytes 9437192 | tf_op jit(solution)/shard_map/ppermute | solution.py:421
  3.3 22.6 %collective-permute-start.4 = (bf16[2048,768]{1,0:T(8,128)(2,1)}, bf16[2048,768]{1,0:T(8,128)(2,1)}, u32[]{:S(2)}, u32[]{:S(2)}) collective-permute-start(bf16[2048,768]{1,0:T(8,128)(2,1)} %bitcast.50), channel_id=1, source_target_pairs={{0,16},{16,0},{32,48},{48,32},{64,80},{80,64},{96,112},{112,96},{1... | collective-permute-start | bytes 9437192 | tf_op jit(solution)/shard_map/ppermute | solution.py:421
  3.5 22.4 %collective-permute-start.5 = (bf16[768,2048]{1,0:T(8,128)(2,1)}, bf16[768,2048]{1,0:T(8,128)(2,1)}, u32[]{:S(2)}, u32[]{:S(2)}) collective-permute-start(bf16[768,2048]{1,0:T(8,128)(2,1)} %bitcast.56), channel_id=1, source_target_pairs={{0,16},{16,0},{32,48},{48,32},{64,80},{80,64},{96,112},{112,96},{1... | collective-permute-start | bytes 9437192 | tf_op jit(solution)/shard_map/ppermute | solution.py:421
  80.8 5.6 %collective-permute-start.6 = (bf16[4,16,2048]{2,1,0:T(8,128)(2,1)S(1)}, bf16[4,16,2048]{2,1,0:T(8,128)(2,1)S(1)}, u32[]{:S(2)}, u32[]{:S(2)}) collective-permute-start(bf16[4,16,2048]{2,1,0:T(8,128)(2,1)S(1)} %mix.3.refs_4_), channel_id=1, source_target_pairs={{0,32},{16,48},{32,0},{48,16},{64,96},{80,112},{96,64},{112,80},{1... | collective-permute-start | bytes 786440 | tf_op jit(solution)/shard_map/ppermute | solution.py:455
  157.5 0.7 collective-permute-start.7
  229.8 10.7 %collective-permute-start.8 = (bf16[4,16,2048]{2,1,0:T(8,128)(2,1)S(1)}, bf16[4,16,2048]{2,1,0:T(8,128)(2,1)S(1)}, u32[]{:S(2)}, u32[]{:S(2)}) collective-permute-start(bf16[4,16,2048]{2,1,0:T(8,128)(2,1)S(1)} %mix.5.refs_6_), channel_id=1, source_target_pairs={{0,32},{16,48},{32,0},{48,16},{64,96},{80,112},{96,64},{112,80},{1... | collective-permute-start | bytes 786440 | tf_op jit(solution)/shard_map/ppermute | solution.py:455
  311.5 8.2 %collective-permute-start.9 = (bf16[4,16,2048]{2,1,0:T(8,128)(2,1)S(1)}, bf16[4,16,2048]{2,1,0:T(8,128)(2,1)S(1)}, u32[]{:S(2)}, u32[]{:S(2)}) collective-permute-start(bf16[4,16,2048]{2,1,0:T(8,128)(2,1)S(1)} %get-tuple-element.110), channel_id=1, source_target_pairs={{0,16},{16,0},{32,48},{48,32},{64,80},{80,64},{96,112},{112,96},{1... | collective-permute-start | bytes 786440 | tf_op jit(solution)/shard_map/ppermute | solution.py:421
where the time goes:
time: 322 us; the launch traced here: 321 us
  blocking collectives  241 us (75%)
  Pallas kernels  50.9 us (16%)
  starting transfers between devices  18.6 us (6%)
  waiting for transfers between devices  10.3 us (3%)
    all_to_all x16, blocking collectives, exchange(): return lax.all_to_all(slots, 'expert', 0, 0, tiled=True)  241 us
    pallas_call x8, Pallas kernels, load_ffn(): pl.pallas_call(kernel, out_shape=(pltpu.VMEM(flat.shape, jnp.bfloat16), *...  46 us
    ppermute x7, starting transfers between devices, swapped(): return lax.ppermute(x, 'pipe', swap)  9.75 us
    ppermute x3, starting transfers between devices, shards(): hidden = lax.ppermute(hidden, 'pipe', relay_pairs(step, stages))  8.88 us
    ppermute x3, waiting for transfers between devices, shards(): hidden = lax.ppermute(hidden, 'pipe', relay_pairs(step, stages))  8.07 us
  transfers between devices with their start and end apart: 10, of which 5 were waited for; matrix products, arithmetic and copies ran while one was open for 0% of the time, Pallas kernels for 0%

commit v1 on v0

--- a/solution.py
+++ b/solution.py
@@ -1,3 +1,5 @@
+import functools
+
 import jax
 import jax.numpy as jnp
 from jax import lax
@@ -7,8 +9,8 @@
 
 H_CUT = 256
 D_CUT = 512
-AHEAD = 3
-STREAMED = (0,)
+AHEAD = 8
+KEPT = (1,)
 K_CUT = 512
 DOWN_PARTS = 3
 SMALL = pltpu.CompilerParams(vmem_limit_bytes=8 * 1024 * 1024)
@@ -28,6 +30,10 @@
 
 def core_of(section_ref):
     return section_ref[0] & 1
+
+
+def working(section_ref, step):
+    return (section_ref[0] >> 1) == step
 
 
 def normalised(hidden, gain_row):
@@ -191,9 +197,10 @@
 
 
 def join_kernel(section_ref, kept_ref, got_ref, out_ref, sems):
+    lane = core_of(section_ref)
     copies = [
-        pltpu.make_async_copy(kept_ref, out_ref.at[:, core_of(section_ref)], sems.at[0]),
-        pltpu.make_async_copy(got_ref, out_ref.at[:, 1 - core_of(section_ref)], sems.at[1]),
+        pltpu.make_async_copy(kept_ref, out_ref.at[:, lane], sems.at[0]),
+        pltpu.make_async_copy(got_ref, out_ref.at[:, 1 - lane], sems.at[1]),
     ]
     for copy in copies:
         copy.start()
@@ -278,42 +285,44 @@
             out_ref[...] = (down_sum[...] + term).astype(jnp.bfloat16)
 
 
-def stream_on_core_1(section_ref, copies):
-    def start():
-        @pl.when(core_of(section_ref) != 0)
-        def _():
-            for copy in copies:
-                copy.start()
-
-    def ready(i):
-        @pl.when(core_of(section_ref) != 0)
-        def _():
-            copies[i].wait()
-
-    return start, ready
-
-
 def first_ffn_kernel(
     section_ref, x_ref, gi, ui, di, gx, ux, dx, out_ref, gate_ref, up_ref, down_ref, gate_next, up_next, down_next,
     active_v, gate_sum, up_sum, down_sum, sems
 ):
     targets = (gate_ref, up_ref, down_ref)
-    start, ready = stream_on_core_1(section_ref, load_copies((gx, ux, dx), targets, sems))
-    copies = load_copies((gx, ux, dx), (gate_next, up_next, down_next), sems)
-    start()
 
     @pl.when(core_of(section_ref) == 0)
     def _():
+        copies = load_copies((gx, ux, dx), (gate_next, up_next, down_next), sems)
         for copy in copies:
             copy.start()
         for copy in copies[:AHEAD]:
             copy.wait()
 
-    streamed_ffn(x_ref, targets, out_ref, active_v, gate_sum, up_sum, down_sum, ready)
-
-    @pl.when(core_of(section_ref) == 0)
-    def _():
+        @pl.when(working(section_ref, 0))
+        def _():
+            ffn_body(x_ref, *targets, out_ref, active_v)
+
         for copy in copies[AHEAD:]:
+            copy.wait()
+
+    @pl.when(core_of(section_ref) != 0)
+    def _():
+        stream_and_run(section_ref, x_ref, (gx, ux, dx), targets, out_ref, active_v, gate_sum, up_sum, down_sum, sems)
+
+
+def stream_and_run(section_ref, x_ref, sources, targets, out_ref, active_v, gate_sum, up_sum, down_sum, sems):
+    copies = load_copies(sources, targets, sems)
+    for copy in copies:
+        copy.start()
+
+    @pl.when(working(section_ref, 0))
+    def _():
+        streamed_ffn(x_ref, targets, out_ref, active_v, gate_sum, up_sum, down_sum, lambda i: copies[i].wait())
+
+    @pl.when(jnp.logical_not(working(section_ref, 0)))
+    def _():
+        for copy in copies:
             copy.wait()
 
 
@@ -322,13 +331,18 @@
     active_v, gate_sum, up_sum, down_sum, sems
 ):
     targets = (gate_ref, up_ref, down_ref)
-    start, ready = stream_on_core_1(section_ref, load_copies((g_h, u_h, d_h), targets, sems))
-    start()
-    streamed_ffn(x_ref, targets, out_ref, active_v, gate_sum, up_sum, down_sum, ready)
+
+    @pl.when(jnp.logical_and(core_of(section_ref) == 0, working(section_ref, 0)))
+    def _():
+        ffn_body(x_ref, *targets, out_ref, active_v)
+
+    @pl.when(core_of(section_ref) != 0)
+    def _():
+        stream_and_run(section_ref, x_ref, (g_h, u_h, d_h), targets, out_ref, active_v, gate_sum, up_sum, down_sum, sems)
 
 
 def later_ffn_kernel(
-    section_ref, x_ref, gi, ui, di, g_h, u_h, d_h, out_ref, gate_ref, up_ref, down_ref,
+    step, section_ref, x_ref, gi, ui, di, g_h, u_h, d_h, out_ref, gate_ref, up_ref, down_ref,
     active_v, gate_sum, up_sum, down_sum, sems
 ):
     @pl.when(core_of(section_ref) != 0)
@@ -339,7 +353,9 @@
         for copy in copies:
             copy.wait()
 
-    ffn_kernel(x_ref, gate_ref, up_ref, down_ref, out_ref, active_v)
+    @pl.when(working(section_ref, step))
+    def _():
+        ffn_body(x_ref, gate_ref, up_ref, down_ref, out_ref, active_v)
 
 
 def ffn_cost(flat, hidden):
@@ -384,7 +400,7 @@
     return produced.reshape(received.shape), weights
 
 
-def ffn_kernel(x_ref, gate_ref, up_ref, down_ref, out_ref, active_v):
+def ffn_body(x_ref, gate_ref, up_ref, down_ref, out_ref, active_v):
     for c in range(gate_ref.shape[1] // H_CUT):
         cut = pl.ds(c * H_CUT, H_CUT)
         gate_part = jnp.dot(x_ref[...], gate_ref[:, cut], preferred_element_type=jnp.float32)
@@ -393,6 +409,29 @@
     down_part(active_v, down_ref, out_ref)
 
 
+def ffn_kernel(step, section_ref, x_ref, gate_ref, up_ref, down_ref, out_ref, active_v):
+    @pl.when(working(section_ref, step))
+    def _():
+        ffn_body(x_ref, gate_ref, up_ref, down_ref, out_ref, active_v)
+
+
+def ffn(step, section_table, received, weights):
+    experts, rows, width = received.shape
+    flat = received.reshape(experts * rows, width)
+    hidden = weights[0].shape[1]
+    produced = pl.pallas_call(
+        functools.partial(ffn_kernel, step),
+        out_shape=pltpu.VMEM(flat.shape, jnp.bfloat16),
+        in_specs=[spec(pltpu.SMEM)] + [spec(pltpu.VMEM)] * 4,
+        out_specs=spec(pltpu.VMEM),
+        scratch_shapes=[pltpu.VMEM((flat.shape[0], hidden), jnp.bfloat16)],
+        compiler_params=SMALL,
+        cost_estimate=ffn_cost(flat, hidden),
+        name="expert_ffn",
+    )(section_table, in_vmem(flat), *[in_vmem(w) for w in weights])
+    return produced.reshape(received.shape)
+
+
 def exchange(slots):
     return lax.all_to_all(slots, "expert", 0, 0, tiled=True)
 
@@ -401,6 +440,8 @@
     place = list(range(stages))
     for x in range(step % 2, stages - 1, 2):
         place[x], place[x + 1] = x + 1, x
+    if step % 2:
+        place[0], place[-1] = stages - 1, 0
     return [(2 * x + c, 2 * place[x] + c) for x in range(stages) for c in range(2)]
 
 
@@ -438,15 +479,21 @@
         if step == 0:
             made, weights = load_ffn(first_ffn_kernel, section_table, received, weights_a, other, True, 1)
             weights_a, weights_b = weights[:3], weights[3:]
+        elif step in KEPT:
+            made = ffn(step, section_table, received, weights_a)
         else:
-            made, weights_a = load_ffn(later_ffn_kernel, section_table, received, weights_a, other, True)
+            kernel = functools.partial(later_ffn_kernel, step)
+            made, weights_a = load_ffn(kernel, section_table, received, weights_a, other, True)
         hidden, sent = small_call(
             between_kernel, "mix_norm_pack", (held, slots), (held,), (ids, scores), (hidden, exchange(made), gains)
         )
         out_a.append(hidden)
         received = exchange(sent)
-        kernel = second_ffn_kernel if step in STREAMED else later_ffn_kernel
-        made, weights_b = load_ffn(kernel, section_table, received, weights_b, own, False)
+        if step == 0:
+            made, weights_b = load_ffn(second_ffn_kernel, section_table, received, weights_b, own, False)
+        else:
+            kernel = functools.partial(later_ffn_kernel, step)
+            made, weights_b = load_ffn(kernel, section_table, received, weights_b, own, False)
         back = exchange(made)
         if step == stages - 1:
             break

time: 322 us -> 314 us (0.975)
  the two profiles are of different devices: /device:TPU:1 before, /device:TPU:7 now
where the time goes in v1:
time: 314 us; the launch traced here: 313 us
  blocking collectives  241 us (77%)
  Pallas kernels  34.4 us (11%)
  starting transfers between devices  22.6 us (7%)
  waiting for transfers between devices  15.1 us (5%)
    all_to_all x16, blocking collectives, exchange(): return lax.all_to_all(slots, 'expert', 0, 0, tiled=True)  241 us
    pallas_call x7, Pallas kernels, load_ffn(): pl.pallas_call(kernel, out_shape=(pltpu.VMEM(flat.shape, jnp.bfloat16), *...  29.5 us
    ppermute x3, waiting for transfers between devices, shards(): hidden = lax.ppermute(hidden, 'pipe', relay_pairs(step, stages))  12.9 us
    ppermute x3, starting transfers between devices, shards(): hidden = lax.ppermute(hidden, 'pipe', relay_pairs(step, stages))  12.2 us
    ppermute x7, starting transfers between devices, swapped(): return lax.ppermute(x, 'pipe', swap)  10.4 us
  transfers between devices with their start and end apart: 10, of which 6 were waited for; matrix products, arithmetic and copies ran while one was open for 0% of the time, Pallas kernels for 0%

profile of v1, /device:TPU:7, one launch (start us, length us, event | category | flops | bytes accessed | tf_op | source)
XLA Modules:
  0.0 313.4 jit_solution(15996531937893964432)
XLA Ops:
  0.0 0.7 collective-permute-start.1
  0.7 0.5 collective-permute-start.2
  1.2 0.8 collective-permute-done.rx_h
  2.0 0.2 collective-permute-done.2.sx_h
  2.2 0.3 collective-permute-start.3
  2.5 0.2 collective-permute-start.4
  2.7 0.3 collective-permute-start.5
  3.1 1.3 slice_norm_pack.1
  4.3 20.7 %all_to_all.80 = bf16[16,16,2048]{2,1,0:T(8,128)(2,1)S(1)} all-to-all(bf16[16,16,2048]{2,1,0:T(8,128)(2,1)S(1)} %get-tuple-element.63), channel_id=1, replica_groups=mesh['pipe'=8,'expert'=16] {'expert'}, dimensions={0} | all-to-all | bytes 2097152 | tf_op jit(solution)/shard_map/all_to_all | solution.py:436
  25.0 3.0 load_expert_ffn.7
  28.1 15.3 %all_to_all.81.returned_ref = bf16[16,16,2048]{2,1,0:T(8,128)(2,1)S(1)} all-to-all(bf16[16,16,2048]{2,1,0:T(8,128)(2,1)S(1)} %bitcast.37), channel_id=1, replica_groups=mesh['pipe'=8,'expert'=16] {'expert'}, dimensions={0} | all-to-all | bytes 2097152 | tf_op jit(solution)/shard_map/all_to_all | solution.py:436
  43.3 0.4 mix_norm_pack.4
  43.7 14.6 %all_to_all.82 = bf16[16,16,2048]{2,1,0:T(8,128)(2,1)S(1)} all-to-all(bf16[16,16,2048]{2,1,0:T(8,128)(2,1)S(1)} %get-tuple-element.70), channel_id=1, replica_groups=mesh['pipe'=8,'expert'=16] {'expert'}, dimensions={0} | all-to-all | bytes 2097152 | tf_op jit(solution)/shard_map/all_to_all | solution.py:436
  58.3 3.8 %load_expert_ffn.8 = (bf16[256,2048]{1,0:T(8,128)(2,1)S(1)}, bf16[2048,768]{1,0:T(8,128)(2,1)S(1)}, bf16[2048,768]{1,0:T(8,128)(2,1)S(1)}, bf16[768,2048]{1,0:T(8,128)(2,1)S(1)}) custom-call(s32[1]{0:T(128)} %bitcast.section_ref, bf16[256,2048]{1,0:T(8,128)(2,1)S(1)} %bitcast.33, ...), custom_call_target="tpu_custom_call", output_to_operand_aliasing={{1}: (2, {}), {2}: (3, {}), {3}: (4, {})} | custom-call | flops 2415919104 | bytes 11534336 | tf_op jit(solution)/shard_map/load_expert_ffn/pallas_call | solution.py:375
  62.1 15.9 %all_to_all.83.returned_ref = bf16[16,16,2048]{2,1,0:T(8,128)(2,1)S(1)} all-to-all(bf16[16,16,2048]{2,1,0:T(8,128)(2,1)S(1)} %bitcast.39), channel_id=1, replica_groups=mesh['pipe'=8,'expert'=16] {'expert'}, dimensions={0} | all-to-all | bytes 2097152 | tf_op jit(solution)/shard_map/all_to_all | solution.py:436
  78.2 0.6 collective-permute-start.6
  78.8 4.7 %collective-permute-done.6.hidden_ref = bf16[4,16,2048]{2,1,0:T(8,128)(2,1)S(1)} collective-permute-done((bf16[4,16,2048]{2,1,0:T(8,128)(2,1)S(1)}, bf16[4,16,2048]{2,1,0:T(8,128)(2,1)S(1)}, u32[]{:S(2)}, u32[]{:S(2)}) %collective-permute-start.6) | collective-permute-done | bytes 262176 | tf_op jit(solution)/shard_map/ppermute | solution.py:502
  83.5 0.2 norm_pack.3
  83.7 15.1 %all_to_all.84 = bf16[16,16,2048]{2,1,0:T(8,128)(2,1)S(1)} all-to-all(bf16[16,16,2048]{2,1,0:T(8,128)(2,1)S(1)} %norm_pack.3), channel_id=1, replica_groups=mesh['pipe'=8,'expert'=16] {'expert'}, dimensions={0} | all-to-all | bytes 2097152 | tf_op jit(solution)/shard_map/all_to_all | solution.py:436
  98.8 14.5 %all_to_all.85.returned_ref = bf16[16,16,2048]{2,1,0:T(8,128)(2,1)S(1)} all-to-all(bf16[16,16,2048]{2,1,0:T(8,128)(2,1)S(1)} %bitcast.36), channel_id=1, replica_groups=mesh['pipe'=8,'expert'=16] {'expert'}, dimensions={0} | all-to-all | bytes 2097152 | tf_op jit(solution)/shard_map/all_to_all | solution.py:436
  113.3 0.4 mix_norm_pack.5
  113.7 14.5 %all_to_all.86 = bf16[16,16,2048]{2,1,0:T(8,128)(2,1)S(1)} all-to-all(bf16[16,16,2048]{2,1,0:T(8,128)(2,1)S(1)} %get-tuple-element.79), channel_id=1, replica_groups=mesh['pipe'=8,'expert'=16] {'expert'}, dimensions={0} | all-to-all | bytes 2097152 | tf_op jit(solution)/shard_map/all_to_all | solution.py:436
  128.2 3.8 %load_expert_ffn.9 = (bf16[256,2048]{1,0:T(8,128)(2,1)S(1)}, bf16[2048,768]{1,0:T(8,128)(2,1)S(1)}, bf16[2048,768]{1,0:T(8,128)(2,1)S(1)}, bf16[768,2048]{1,0:T(8,128)(2,1)S(1)}) custom-call(s32[1]{0:T(128)} %bitcast.section_ref, bf16[256,2048]{1,0:T(8,128)(2,1)S(1)} %bitcast.30, ...), custom_call_target="tpu_custom_call", output_to_operand_aliasing={{1}: (2, {}), {2}: (3, {}), {3}: (4, {})} | custom-call | flops 2415919104 | bytes 11534336 | tf_op jit(solution)/shard_map/load_expert_ffn/pallas_call | solution.py:375
  132.0 14.6 %all_to_all.87.returned_ref = bf16[16,16,2048]{2,1,0:T(8,128)(2,1)S(1)} all-to-all(bf16[16,16,2048]{2,1,0:T(8,128)(2,1)S(1)} %bitcast.40), channel_id=1, replica_groups=mesh['pipe'=8,'expert'=16] {'expert'}, dimensions={0} | all-to-all | bytes 2097152 | tf_op jit(solution)/shard_map/all_to_all | solution.py:436
  146.7 2.2 collective-permute-start.7
  148.9 4.5 %collective-permute-done.7.hidden_ref = bf16[4,16,2048]{2,1,0:T(8,128)(2,1)S(1)} collective-permute-done((bf16[4,16,2048]{2,1,0:T(8,128)(2,1)S(1)}, bf16[4,16,2048]{2,1,0:T(8,128)(2,1)S(1)}, u32[]{:S(2)}, u32[]{:S(2)}) %collective-permute-start.7) | collective-permute-done | bytes 262176 | tf_op jit(solution)/shard_map/ppermute | solution.py:502
  153.4 0.2 norm_pack.4
  153.7 14.5 %all_to_all.88 = bf16[16,16,2048]{2,1,0:T(8,128)(2,1)S(1)} all-to-all(bf16[16,16,2048]{2,1,0:T(8,128)(2,1)S(1)} %norm_pack.4), channel_id=1, replica_groups=mesh['pipe'=8,'expert'=16] {'expert'}, dimensions={0} | all-to-all | bytes 2097152 | tf_op jit(solution)/shard_map/all_to_all | solution.py:436
  168.1 3.0 load_expert_ffn.10
  171.1 14.5 %all_to_all.89.returned_ref = bf16[16,16,2048]{2,1,0:T(8,128)(2,1)S(1)} all-to-all(bf16[16,16,2048]{2,1,0:T(8,128)(2,1)S(1)} %bitcast.41), channel_id=1, replica_groups=mesh['pipe'=8,'expert'=16] {'expert'}, dimensions={0} | all-to-all | bytes 2097152 | tf_op jit(solution)/shard_map/all_to_all | solution.py:436
  185.6 0.4 mix_norm_pack.6
  186.0 14.5 %all_to_all.90 = bf16[16,16,2048]{2,1,0:T(8,128)(2,1)S(1)} all-to-all(bf16[16,16,2048]{2,1,0:T(8,128)(2,1)S(1)} %get-tuple-element.86), channel_id=1, replica_groups=mesh['pipe'=8,'expert'=16] {'expert'}, dimensions={0} | all-to-all | bytes 2097152 | tf_op jit(solution)/shard_map/all_to_all | solution.py:436
  200.4 3.8 %load_expert_ffn.11 = (bf16[256,2048]{1,0:T(8,128)(2,1)S(1)}, bf16[2048,768]{1,0:T(8,128)(2,1)S(1)}, bf16[2048,768]{1,0:T(8,128)(2,1)S(1)}, bf16[768,2048]{1,0:T(8,128)(2,1)S(1)}) custom-call(s32[1]{0:T(128)} %bitcast.section_ref, bf16[256,2048]{1,0:T(8,128)(2,1)S(1)} %bitcast.31, ...), custom_call_target="tpu_custom_call", output_to_operand_aliasing={{1}: (2, {}), {2}: (3, {}), {3}: (4, {})} | custom-call | flops 2415919104 | bytes 11534336 | tf_op jit(solution)/shard_map/load_expert_ffn/pallas_call | solution.py:375
  204.2 14.5 %all_to_all.91.returned_ref = bf16[16,16,2048]{2,1,0:T(8,128)(2,1)S(1)} all-to-all(bf16[16,16,2048]{2,1,0:T(8,128)(2,1)S(1)} %bitcast.42), channel_id=1, replica_groups=mesh['pipe'=8,'expert'=16] {'expert'}, dimensions={0} | all-to-all | bytes 2097152 | tf_op jit(solution)/shard_map/all_to_all | solution.py:436
  218.9 9.4 %collective-permute-start.8 = (bf16[4,16,2048]{2,1,0:T(8,128)(2,1)S(1)}, bf16[4,16,2048]{2,1,0:T(8,128)(2,1)S(1)}, u32[]{:S(2)}, u32[]{:S(2)}) collective-permute-start(bf16[4,16,2048]{2,1,0:T(8,128)(2,1)S(1)} %mix.5.refs_6_), channel_id=1, source_target_pairs={{0,32},{16,48},{32,0},{48,16},{64,96},{80,112},{96,64},{112,80},{1... | collective-permute-start | bytes 786440 | tf_op jit(solution)/shard_map/ppermute | solution.py:502
  228.3 3.8 %collective-permute-done.8.hidden_ref = bf16[4,16,2048]{2,1,0:T(8,128)(2,1)S(1)} collective-permute-done((bf16[4,16,2048]{2,1,0:T(8,128)(2,1)S(1)}, bf16[4,16,2048]{2,1,0:T(8,128)(2,1)S(1)}, u32[]{:S(2)}, u32[]{:S(2)}) %collective-permute-start.8) | collective-permute-done | bytes 262176 | tf_op jit(solution)/shard_map/ppermute | solution.py:502
  232.1 0.2 norm_pack.5
  232.3 14.5 %all_to_all.92 = bf16[16,16,2048]{2,1,0:T(8,128)(2,1)S(1)} all-to-all(bf16[16,16,2048]{2,1,0:T(8,128)(2,1)S(1)} %norm_pack.5), channel_id=1, replica_groups=mesh['pipe'=8,'expert'=16] {'expert'}, dimensions={0} | all-to-all | bytes 2097152 | tf_op jit(solution)/shard_map/all_to_all | solution.py:436
  246.8 5.6 %load_expert_ffn.12 = (bf16[256,2048]{1,0:T(8,128)(2,1)S(1)}, bf16[2048,768]{1,0:T(8,128)(2,1)S(1)}, bf16[2048,768]{1,0:T(8,128)(2,1)S(1)}, bf16[768,2048]{1,0:T(8,128)(2,1)S(1)}) custom-call(s32[1]{0:T(128)} %bitcast.section_ref, bf16[256,2048]{1,0:T(8,128)(2,1)S(1)} %bitcast.29, ...), custom_call_target="tpu_custom_call", output_to_operand_aliasing={{1}: (2, {}), {2}: (3, {}), {3}: (4, {})} | custom-call | flops 2415919104 | bytes 11534336 | tf_op jit(solution)/shard_map/load_expert_ffn/pallas_call | solution.py:375
  252.4 14.5 %all_to_all.93.returned_ref = bf16[16,16,2048]{2,1,0:T(8,128)(2,1)S(1)} all-to-all(bf16[16,16,2048]{2,1,0:T(8,128)(2,1)S(1)} %bitcast.38), channel_id=1, replica_groups=mesh['pipe'=8,'expert'=16] {'expert'}, dimensions={0} | all-to-all | bytes 2097152 | tf_op jit(solution)/shard_map/all_to_all | solution.py:436
  266.9 0.4 mix_norm_pack.7
  267.2 14.5 %all_to_all.94 = bf16[16,16,2048]{2,1,0:T(8,128)(2,1)S(1)} all-to-all(bf16[16,16,2048]{2,1,0:T(8,128)(2,1)S(1)} %get-tuple-element.96), channel_id=1, replica_groups=mesh['pipe'=8,'expert'=16] {'expert'}, dimensions={0} | all-to-all | bytes 2097152 | tf_op jit(solution)/shard_map/all_to_all | solution.py:436
  281.7 6.4 %load_expert_ffn.13 = (bf16[256,2048]{1,0:T(8,128)(2,1)S(1)}, bf16[2048,768]{1,0:T(8,128)(2,1)S(1)}, bf16[2048,768]{1,0:T(8,128)(2,1)S(1)}, bf16[768,2048]{1,0:T(8,128)(2,1)S(1)}) custom-call(s32[1]{0:T(128)} %bitcast.section_ref, bf16[256,2048]{1,0:T(8,128)(2,1)S(1)} %bitcast.32, ...), custom_call_target="tpu_custom_call", output_to_operand_aliasing={{1}: (2, {}), {2}: (3, {}), {3}: (4, {})} | custom-call | flops 2415919104 | bytes 11534336 | tf_op jit(solution)/shard_map/load_expert_ffn/pallas_call | solution.py:375
  288.1 14.5 %all_to_all.95.returned_ref = bf16[16,16,2048]{2,1,0:T(8,128)(2,1)S(1)} all-to-all(bf16[16,16,2048]{2,1,0:T(8,128)(2,1)S(1)} %bitcast.43), channel_id=1, replica_groups=mesh['pipe'=8,'expert'=16] {'expert'}, dimensions={0} | all-to-all | bytes 2097152 | tf_op jit(solution)/shard_map/all_to_all | solution.py:436
  302.6 0.3 mix_choose.1
  302.9 8.3 %collective-permute-start.9 = (bf16[4,16,2048]{2,1,0:T(8,128)(2,1)S(1)}, bf16[4,16,2048]{2,1,0:T(8,128)(2,1)S(1)}, u32[]{:S(2)}, u32[]{:S(2)}) collective-permute-start(bf16[4,16,2048]{2,1,0:T(8,128)(2,1)S(1)} %get-tuple-element.102), channel_id=1, source_target_pairs={{0,16},{16,0},{32,48},{48,32},{64,80},{80,64},{96,112},{112,96},{1... | collective-permute-start | bytes 786440 | tf_op jit(solution)/shard_map/ppermute | solution.py:462
  311.2 1.2 collective-permute-done.9.got_ref
  312.4 0.8 join_rows.1
  (9 shorter events, 0.5 us)
Async XLA Ops:
  0.0 2.2 collective-permute-start.1
  0.7 1.4 collective-permute-start
  0.7 1.5 collective-permute-start.2
  2.2 22.8 %collective-permute-start.3 = (bf16[2048,768]{1,0:T(8,128)(2,1)}, bf16[2048,768]{1,0:T(8,128)(2,1)S(1)}, u32[]{:S(2)}, u32[]{:S(2)}) collective-permute-start(bf16[2048,768]{1,0:T(8,128)(2,1)} %bitcast.44), channel_id=1, source_target_pairs={{0,16},{16,0},{32,48},{48,32},{64,80},{80,64},{96,112},{112,96},{1... | collective-permute-start | bytes 9437192 | tf_op jit(solution)/shard_map/ppermute | solution.py:462
  2.5 22.5 %collective-permute-start.4 = (bf16[2048,768]{1,0:T(8,128)(2,1)}, bf16[2048,768]{1,0:T(8,128)(2,1)}, u32[]{:S(2)}, u32[]{:S(2)}) collective-permute-start(bf16[2048,768]{1,0:T(8,128)(2,1)} %bitcast.50), channel_id=1, source_target_pairs={{0,16},{16,0},{32,48},{48,32},{64,80},{80,64},{96,112},{112,96},{1... | collective-permute-start | bytes 9437192 | tf_op jit(solution)/shard_map/ppermute | solution.py:462
  2.7 22.3 %collective-permute-start.5 = (bf16[768,2048]{1,0:T(8,128)(2,1)}, bf16[768,2048]{1,0:T(8,128)(2,1)}, u32[]{:S(2)}, u32[]{:S(2)}) collective-permute-start(bf16[768,2048]{1,0:T(8,128)(2,1)} %bitcast.56), channel_id=1, source_target_pairs={{0,16},{16,0},{32,48},{48,32},{64,80},{80,64},{96,112},{112,96},{1... | collective-permute-start | bytes 9437192 | tf_op jit(solution)/shard_map/ppermute | solution.py:462
  78.2 5.3 %collective-permute-start.6 = (bf16[4,16,2048]{2,1,0:T(8,128)(2,1)S(1)}, bf16[4,16,2048]{2,1,0:T(8,128)(2,1)S(1)}, u32[]{:S(2)}, u32[]{:S(2)}) collective-permute-start(bf16[4,16,2048]{2,1,0:T(8,128)(2,1)S(1)} %mix.3.refs_4_), channel_id=1, source_target_pairs={{0,32},{16,48},{32,0},{48,16},{64,96},{80,112},{96,64},{112,80},{1... | collective-permute-start | bytes 786440 | tf_op jit(solution)/shard_map/ppermute | solution.py:502
  146.7 6.8 %collective-permute-start.7 = (bf16[4,16,2048]{2,1,0:T(8,128)(2,1)S(1)}, bf16[4,16,2048]{2,1,0:T(8,128)(2,1)S(1)}, u32[]{:S(2)}, u32[]{:S(2)}) collective-permute-start(bf16[4,16,2048]{2,1,0:T(8,128)(2,1)S(1)} %mix.4.refs_5_), channel_id=1, source_target_pairs={{0,96},{16,112},{32,64},{48,80},{64,32},{80,48},{96,0},{112,16},{1... | collective-permute-start | bytes 786440 | tf_op jit(solution)/shard_map/ppermute | solution.py:502
  218.9 13.1 %collective-permute-start.8 = (bf16[4,16,2048]{2,1,0:T(8,128)(2,1)S(1)}, bf16[4,16,2048]{2,1,0:T(8,128)(2,1)S(1)}, u32[]{:S(2)}, u32[]{:S(2)}) collective-permute-start(bf16[4,16,2048]{2,1,0:T(8,128)(2,1)S(1)} %mix.5.refs_6_), channel_id=1, source_target_pairs={{0,32},{16,48},{32,0},{48,16},{64,96},{80,112},{96,64},{112,80},{1... | collective-permute-start | bytes 786440 | tf_op jit(solution)/shard_map/ppermute | solution.py:502
  302.9 9.5 %collective-permute-start.9 = (bf16[4,16,2048]{2,1,0:T(8,128)(2,1)S(1)}, bf16[4,16,2048]{2,1,0:T(8,128)(2,1)S(1)}, u32[]{:S(2)}, u32[]{:S(2)}) collective-permute-start(bf16[4,16,2048]{2,1,0:T(8,128)(2,1)S(1)} %get-tuple-element.102), channel_id=1, source_target_pairs={{0,16},{16,0},{32,48},{48,32},{64,80},{80,64},{96,112},{112,96},{1... | collective-permute-start | bytes 786440 | tf_op jit(solution)/shard_map/ppermute | solution.py:462

commit v2 on v1

--- a/solution.py
+++ b/solution.py
@@ -9,7 +9,7 @@
 
 H_CUT = 256
 D_CUT = 512
-AHEAD = 8
+AHEAD = 10
 KEPT = (1,)
 K_CUT = 512
 DOWN_PARTS = 3
@@ -166,21 +166,28 @@
 
 
 def finish_kernel(section_ref, ids_ref, scores_ref, hidden_ref, returned_ref, *refs):
-    earlier, (kept_ref, sent_ref, last_ref, sems) = refs[:-4], refs[-4:]
+    earlier, (kept_ref, sent_ref, sems) = refs[:-3], refs[-3:]
     stages = (len(earlier) + 1) // 2
-    for block in range(hidden_ref.shape[0]):
-        last_ref[block] = mixed(1, ids_ref, scores_ref, hidden_ref, returned_ref, block)
-    results_a, results_b = earlier[:stages], (*earlier[stages:], last_ref)
+    last = stages - 1
+    results_a, results_b = earlier[:stages], earlier[stages:]
+    ways = ((0, (kept_ref, sent_ref)), (1, (sent_ref, kept_ref)))
     for step in range(stages):
-        for core, targets in ((0, (kept_ref, sent_ref)), (1, (sent_ref, kept_ref))):
+        for core, (target_a, target_b) in ways:
 
             @pl.when(section_ref[0] == 2 * step + core)
             def _():
-                for i, source in enumerate((results_a[step], results_b[step])):
-                    pltpu.make_async_copy(source, targets[i], sems.at[i]).start()
-
-    for i, target in enumerate((kept_ref, sent_ref)):
-        pltpu.make_async_copy(results_a[0], target, sems.at[i]).wait()
+                pltpu.make_async_copy(results_a[step], target_a, sems.at[0]).start()
+                if step < last:
+                    pltpu.make_async_copy(results_b[step], target_b, sems.at[1]).start()
+                else:
+                    for block in range(hidden_ref.shape[0]):
+                        target_b[block] = mixed(1, ids_ref, scores_ref, hidden_ref, returned_ref, block)
+
+    pltpu.make_async_copy(results_a[0], kept_ref, sems.at[0]).wait()
+
+    @pl.when(section_ref[0] < 2 * last)
+    def _():
+        pltpu.make_async_copy(results_a[0], sent_ref, sems.at[1]).wait()
 
 
 def finish(section_table, ids, scores, hidden, returned, earlier):
@@ -190,7 +197,7 @@
         out_shape=(pltpu.VMEM(held, jnp.bfloat16),) * 2,
         in_specs=[spec(pltpu.SMEM)] * 3 + [spec(pltpu.VMEM)] * 2 + [spec(pl.ANY)] * len(earlier),
         out_specs=(spec(pltpu.VMEM),) * 2,
-        scratch_shapes=[pltpu.VMEM(held, jnp.bfloat16), pltpu.SemaphoreType.DMA((2,))],
+        scratch_shapes=[pltpu.SemaphoreType.DMA((2,))],
         compiler_params=SMALL,
         name="mix_choose",
     )(section_table, ids, scores, in_vmem(hidden), in_vmem(returned), *earlier)

time: 314 us -> 317 us (level)
  no operation moved by 1% of the time
where the time goes in v2:
time: 317 us
  blocking collectives  242 us (76%)
  Pallas kernels  34.3 us (11%)
  starting transfers between devices  25 us (8%)
  waiting for transfers between devices  15.2 us (5%)
    all_to_all x16, blocking collectives, exchange(): return lax.all_to_all(slots, 'expert', 0, 0, tiled=True)  242 us
    pallas_call x7, Pallas kernels, load_ffn(): pl.pallas_call(kernel, out_shape=(pltpu.VMEM(flat.shape, jnp.bfloat16), *...  29.5 us
    ppermute x3, waiting for transfers between devices, shards(): hidden = lax.ppermute(hidden, 'pipe', relay_pairs(step, stages))  13 us
    ppermute x3, starting transfers between devices, shards(): hidden = lax.ppermute(hidden, 'pipe', relay_pairs(step, stages))  12.5 us
    ppermute x7, starting transfers between devices, swapped(): return lax.ppermute(x, 'pipe', swap)  12.4 us
  transfers between devices with their start and end apart: 10, of which 6 were waited for; matrix products, arithmetic and copies ran while one was open for 0% of the time, Pallas kernels for 0%

profile of v2, /device:TPU:7, one launch (start us, length us, event | category | flops | bytes accessed | tf_op | source)
XLA Modules:
  0.0 316.7 jit_solution(14937671032892708032)
XLA Ops:
  0.0 0.7 collective-permute-start.1
  0.7 0.5 collective-permute-start.2
  1.2 0.8 collective-permute-done.rx_h
  2.0 0.2 collective-permute-done.2.sx_h
  2.2 0.3 collective-permute-start.3
  2.5 0.2 collective-permute-start.4
  2.7 0.3 collective-permute-start.5
  3.1 1.3 slice_norm_pack.1
  4.3 20.7 %all_to_all.80 = bf16[16,16,2048]{2,1,0:T(8,128)(2,1)S(1)} all-to-all(bf16[16,16,2048]{2,1,0:T(8,128)(2,1)S(1)} %get-tuple-element.63), channel_id=1, replica_groups=mesh['pipe'=8,'expert'=16] {'expert'}, dimensions={0} | all-to-all | bytes 2097152 | tf_op jit(solution)/shard_map/all_to_all | solution.py:443
  25.0 3.0 load_expert_ffn.7
  28.1 15.3 %all_to_all.81.returned_ref = bf16[16,16,2048]{2,1,0:T(8,128)(2,1)S(1)} all-to-all(bf16[16,16,2048]{2,1,0:T(8,128)(2,1)S(1)} %bitcast.37), channel_id=1, replica_groups=mesh['pipe'=8,'expert'=16] {'expert'}, dimensions={0} | all-to-all | bytes 2097152 | tf_op jit(solution)/shard_map/all_to_all | solution.py:443
  43.3 0.4 mix_norm_pack.4
  43.7 14.6 %all_to_all.82 = bf16[16,16,2048]{2,1,0:T(8,128)(2,1)S(1)} all-to-all(bf16[16,16,2048]{2,1,0:T(8,128)(2,1)S(1)} %get-tuple-element.70), channel_id=1, replica_groups=mesh['pipe'=8,'expert'=16] {'expert'}, dimensions={0} | all-to-all | bytes 2097152 | tf_op jit(solution)/shard_map/all_to_all | solution.py:443
  58.3 3.8 %load_expert_ffn.8 = (bf16[256,2048]{1,0:T(8,128)(2,1)S(1)}, bf16[2048,768]{1,0:T(8,128)(2,1)S(1)}, bf16[2048,768]{1,0:T(8,128)(2,1)S(1)}, bf16[768,2048]{1,0:T(8,128)(2,1)S(1)}) custom-call(s32[1]{0:T(128)} %bitcast.section_ref, bf16[256,2048]{1,0:T(8,128)(2,1)S(1)} %bitcast.33, ...), custom_call_target="tpu_custom_call", output_to_operand_aliasing={{1}: (2, {}), {2}: (3, {}), {3}: (4, {})} | custom-call | flops 2415919104 | bytes 11534336 | tf_op jit(solution)/shard_map/load_expert_ffn/pallas_call | solution.py:382
  62.1 15.9 %all_to_all.83.returned_ref = bf16[16,16,2048]{2,1,0:T(8,128)(2,1)S(1)} all-to-all(bf16[16,16,2048]{2,1,0:T(8,128)(2,1)S(1)} %bitcast.39), channel_id=1, replica_groups=mesh['pipe'=8,'expert'=16] {'expert'}, dimensions={0} | all-to-all | bytes 2097152 | tf_op jit(solution)/shard_map/all_to_all | solution.py:443
  78.2 0.6 collective-permute-start.6
  78.8 4.7 %collective-permute-done.6.hidden_ref = bf16[4,16,2048]{2,1,0:T(8,128)(2,1)S(1)} collective-permute-done((bf16[4,16,2048]{2,1,0:T(8,128)(2,1)S(1)}, bf16[4,16,2048]{2,1,0:T(8,128)(2,1)S(1)}, u32[]{:S(2)}, u32[]{:S(2)}) %collective-permute-start.6) | collective-permute-done | bytes 262176 | tf_op jit(solution)/shard_map/ppermute | solution.py:509
  83.5 0.2 norm_pack.3
  83.7 15.1 %all_to_all.84 = bf16[16,16,2048]{2,1,0:T(8,128)(2,1)S(1)} all-to-all(bf16[16,16,2048]{2,1,0:T(8,128)(2,1)S(1)} %norm_pack.3), channel_id=1, replica_groups=mesh['pipe'=8,'expert'=16] {'expert'}, dimensions={0} | all-to-all | bytes 2097152 | tf_op jit(solution)/shard_map/all_to_all | solution.py:443
  98.8 14.5 %all_to_all.85.returned_ref = bf16[16,16,2048]{2,1,0:T(8,128)(2,1)S(1)} all-to-all(bf16[16,16,2048]{2,1,0:T(8,128)(2,1)S(1)} %bitcast.36), channel_id=1, replica_groups=mesh['pipe'=8,'expert'=16] {'expert'}, dimensions={0} | all-to-all | bytes 2097152 | tf_op jit(solution)/shard_map/all_to_all | solution.py:443
  113.3 0.4 mix_norm_pack.5
  113.7 14.5 %all_to_all.86 = bf16[16,16,2048]{2,1,0:T(8,128)(2,1)S(1)} all-to-all(bf16[16,16,2048]{2,1,0:T(8,128)(2,1)S(1)} %get-tuple-element.79), channel_id=1, replica_groups=mesh['pipe'=8,'expert'=16] {'expert'}, dimensions={0} | all-to-all | bytes 2097152 | tf_op jit(solution)/shard_map/all_to_all | solution.py:443
  128.2 3.8 %load_expert_ffn.9 = (bf16[256,2048]{1,0:T(8,128)(2,1)S(1)}, bf16[2048,768]{1,0:T(8,128)(2,1)S(1)}, bf16[2048,768]{1,0:T(8,128)(2,1)S(1)}, bf16[768,2048]{1,0:T(8,128)(2,1)S(1)}) custom-call(s32[1]{0:T(128)} %bitcast.section_ref, bf16[256,2048]{1,0:T(8,128)(2,1)S(1)} %bitcast.30, ...), custom_call_target="tpu_custom_call", output_to_operand_aliasing={{1}: (2, {}), {2}: (3, {}), {3}: (4, {})} | custom-call | flops 2415919104 | bytes 11534336 | tf_op jit(solution)/shard_map/load_expert_ffn/pallas_call | solution.py:382
  132.0 14.6 %all_to_all.87.returned_ref = bf16[16,16,2048]{2,1,0:T(8,128)(2,1)S(1)} all-to-all(bf16[16,16,2048]{2,1,0:T(8,128)(2,1)S(1)} %bitcast.40), channel_id=1, replica_groups=mesh['pipe'=8,'expert'=16] {'expert'}, dimensions={0} | all-to-all | bytes 2097152 | tf_op jit(solution)/shard_map/all_to_all | solution.py:443
  146.7 2.2 collective-permute-start.7
  148.9 4.5 %collective-permute-done.7.hidden_ref = bf16[4,16,2048]{2,1,0:T(8,128)(2,1)S(1)} collective-permute-done((bf16[4,16,2048]{2,1,0:T(8,128)(2,1)S(1)}, bf16[4,16,2048]{2,1,0:T(8,128)(2,1)S(1)}, u32[]{:S(2)}, u32[]{:S(2)}) %collective-permute-start.7) | collective-permute-done | bytes 262176 | tf_op jit(solution)/shard_map/ppermute | solution.py:509
  153.4 0.2 norm_pack.4
  153.7 14.5 %all_to_all.88 = bf16[16,16,2048]{2,1,0:T(8,128)(2,1)S(1)} all-to-all(bf16[16,16,2048]{2,1,0:T(8,128)(2,1)S(1)} %norm_pack.4), channel_id=1, replica_groups=mesh['pipe'=8,'expert'=16] {'expert'}, dimensions={0} | all-to-all | bytes 2097152 | tf_op jit(solution)/shard_map/all_to_all | solution.py:443
  168.1 3.0 load_expert_ffn.10
  171.1 14.5 %all_to_all.89.returned_ref = bf16[16,16,2048]{2,1,0:T(8,128)(2,1)S(1)} all-to-all(bf16[16,16,2048]{2,1,0:T(8,128)(2,1)S(1)} %bitcast.41), channel_id=1, replica_groups=mesh['pipe'=8,'expert'=16] {'expert'}, dimensions={0} | all-to-all | bytes 2097152 | tf_op jit(solution)/shard_map/all_to_all | solution.py:443
  185.6 0.4 mix_norm_pack.6
  186.0 14.4 %all_to_all.90 = bf16[16,16,2048]{2,1,0:T(8,128)(2,1)S(1)} all-to-all(bf16[16,16,2048]{2,1,0:T(8,128)(2,1)S(1)} %get-tuple-element.86), channel_id=1, replica_groups=mesh['pipe'=8,'expert'=16] {'expert'}, dimensions={0} | all-to-all | bytes 2097152 | tf_op jit(solution)/shard_map/all_to_all | solution.py:443
  200.4 3.8 %load_expert_ffn.11 = (bf16[256,2048]{1,0:T(8,128)(2,1)S(1)}, bf16[2048,768]{1,0:T(8,128)(2,1)S(1)}, bf16[2048,768]{1,0:T(8,128)(2,1)S(1)}, bf16[768,2048]{1,0:T(8,128)(2,1)S(1)}) custom-call(s32[1]{0:T(128)} %bitcast.section_ref, bf16[256,2048]{1,0:T(8,128)(2,1)S(1)} %bitcast.31, ...), custom_call_target="tpu_custom_call", output_to_operand_aliasing={{1}: (2, {}), {2}: (3, {}), {3}: (4, {})} | custom-call | flops 2415919104 | bytes 11534336 | tf_op jit(solution)/shard_map/load_expert_ffn/pallas_call | solution.py:382
  204.2 14.6 %all_to_all.91.returned_ref = bf16[16,16,2048]{2,1,0:T(8,128)(2,1)S(1)} all-to-all(bf16[16,16,2048]{2,1,0:T(8,128)(2,1)S(1)} %bitcast.42), channel_id=1, replica_groups=mesh['pipe'=8,'expert'=16] {'expert'}, dimensions={0} | all-to-all | bytes 2097152 | tf_op jit(solution)/shard_map/all_to_all | solution.py:443
  218.9 9.7 %collective-permute-start.8 = (bf16[4,16,2048]{2,1,0:T(8,128)(2,1)S(1)}, bf16[4,16,2048]{2,1,0:T(8,128)(2,1)S(1)}, u32[]{:S(2)}, u32[]{:S(2)}) collective-permute-start(bf16[4,16,2048]{2,1,0:T(8,128)(2,1)S(1)} %mix.5.refs_6_), channel_id=1, source_target_pairs={{0,32},{16,48},{32,0},{48,16},{64,96},{80,112},{96,64},{112,80},{1... | collective-permute-start | bytes 786440 | tf_op jit(solution)/shard_map/ppermute | solution.py:509
  228.6 3.8 %collective-permute-done.8.hidden_ref = bf16[4,16,2048]{2,1,0:T(8,128)(2,1)S(1)} collective-permute-done((bf16[4,16,2048]{2,1,0:T(8,128)(2,1)S(1)}, bf16[4,16,2048]{2,1,0:T(8,128)(2,1)S(1)}, u32[]{:S(2)}, u32[]{:S(2)}) %collective-permute-start.8) | collective-permute-done | bytes 262176 | tf_op jit(solution)/shard_map/ppermute | solution.py:509
  232.4 0.2 norm_pack.5
  232.6 14.5 %all_to_all.92 = bf16[16,16,2048]{2,1,0:T(8,128)(2,1)S(1)} all-to-all(bf16[16,16,2048]{2,1,0:T(8,128)(2,1)S(1)} %norm_pack.5), channel_id=1, replica_groups=mesh['pipe'=8,'expert'=16] {'expert'}, dimensions={0} | all-to-all | bytes 2097152 | tf_op jit(solution)/shard_map/all_to_all | solution.py:443
  247.1 5.6 %load_expert_ffn.12 = (bf16[256,2048]{1,0:T(8,128)(2,1)S(1)}, bf16[2048,768]{1,0:T(8,128)(2,1)S(1)}, bf16[2048,768]{1,0:T(8,128)(2,1)S(1)}, bf16[768,2048]{1,0:T(8,128)(2,1)S(1)}) custom-call(s32[1]{0:T(128)} %bitcast.section_ref, bf16[256,2048]{1,0:T(8,128)(2,1)S(1)} %bitcast.29, ...), custom_call_target="tpu_custom_call", output_to_operand_aliasing={{1}: (2, {}), {2}: (3, {}), {3}: (4, {})} | custom-call | flops 2415919104 | bytes 11534336 | tf_op jit(solution)/shard_map/load_expert_ffn/pallas_call | solution.py:382
  252.7 14.5 %all_to_all.93.returned_ref = bf16[16,16,2048]{2,1,0:T(8,128)(2,1)S(1)} all-to-all(bf16[16,16,2048]{2,1,0:T(8,128)(2,1)S(1)} %bitcast.38), channel_id=1, replica_groups=mesh['pipe'=8,'expert'=16] {'expert'}, dimensions={0} | all-to-all | bytes 2097152 | tf_op jit(solution)/shard_map/all_to_all | solution.py:443
  267.2 0.4 mix_norm_pack.7
  267.5 15.5 %all_to_all.94 = bf16[16,16,2048]{2,1,0:T(8,128)(2,1)S(1)} all-to-all(bf16[16,16,2048]{2,1,0:T(8,128)(2,1)S(1)} %get-tuple-element.96), channel_id=1, replica_groups=mesh['pipe'=8,'expert'=16] {'expert'}, dimensions={0} | all-to-all | bytes 2097152 | tf_op jit(solution)/shard_map/all_to_all | solution.py:443
  283.1 6.4 %load_expert_ffn.13 = (bf16[256,2048]{1,0:T(8,128)(2,1)S(1)}, bf16[2048,768]{1,0:T(8,128)(2,1)S(1)}, bf16[2048,768]{1,0:T(8,128)(2,1)S(1)}, bf16[768,2048]{1,0:T(8,128)(2,1)S(1)}) custom-call(s32[1]{0:T(128)} %bitcast.section_ref, bf16[256,2048]{1,0:T(8,128)(2,1)S(1)} %bitcast.32, ...), custom_call_target="tpu_custom_call", output_to_operand_aliasing={{1}: (2, {}), {2}: (3, {}), {3}: (4, {})} | custom-call | flops 2415919104 | bytes 11534336 | tf_op jit(solution)/shard_map/load_expert_ffn/pallas_call | solution.py:382
  289.5 14.5 %all_to_all.95.returned_ref = bf16[16,16,2048]{2,1,0:T(8,128)(2,1)S(1)} all-to-all(bf16[16,16,2048]{2,1,0:T(8,128)(2,1)S(1)} %bitcast.43), channel_id=1, replica_groups=mesh['pipe'=8,'expert'=16] {'expert'}, dimensions={0} | all-to-all | bytes 2097152 | tf_op jit(solution)/shard_map/all_to_all | solution.py:443
  304.0 0.2 mix_choose.1
  304.2 10.4 %collective-permute-start.9 = (bf16[4,16,2048]{2,1,0:T(8,128)(2,1)S(1)}, bf16[4,16,2048]{2,1,0:T(8,128)(2,1)S(1)}, u32[]{:S(2)}, u32[]{:S(2)}) collective-permute-start(bf16[4,16,2048]{2,1,0:T(8,128)(2,1)S(1)} %get-tuple-element.102), channel_id=1, source_target_pairs={{0,16},{16,0},{32,48},{48,32},{64,80},{80,64},{96,112},{112,96},{1... | collective-permute-start | bytes 786440 | tf_op jit(solution)/shard_map/ppermute | solution.py:469
  314.6 1.2 collective-permute-done.9.got_ref
  315.7 0.8 join_rows.1
  (9 shorter events, 0.5 us)
Async XLA Ops:
  0.0 2.2 collective-permute-start.1
  0.7 1.4 collective-permute-start
  0.7 1.5 collective-permute-start.2
  2.2 22.8 %collective-permute-start.3 = (bf16[2048,768]{1,0:T(8,128)(2,1)}, bf16[2048,768]{1,0:T(8,128)(2,1)S(1)}, u32[]{:S(2)}, u32[]{:S(2)}) collective-permute-start(bf16[2048,768]{1,0:T(8,128)(2,1)} %bitcast.44), channel_id=1, source_target_pairs={{0,16},{16,0},{32,48},{48,32},{64,80},{80,64},{96,112},{112,96},{1... | collective-permute-start | bytes 9437192 | tf_op jit(solution)/shard_map/ppermute | solution.py:469
  2.5 22.5 %collective-permute-start.4 = (bf16[2048,768]{1,0:T(8,128)(2,1)}, bf16[2048,768]{1,0:T(8,128)(2,1)}, u32[]{:S(2)}, u32[]{:S(2)}) collective-permute-start(bf16[2048,768]{1,0:T(8,128)(2,1)} %bitcast.50), channel_id=1, source_target_pairs={{0,16},{16,0},{32,48},{48,32},{64,80},{80,64},{96,112},{112,96},{1... | collective-permute-start | bytes 9437192 | tf_op jit(solution)/shard_map/ppermute | solution.py:469
  2.7 22.3 %collective-permute-start.5 = (bf16[768,2048]{1,0:T(8,128)(2,1)}, bf16[768,2048]{1,0:T(8,128)(2,1)}, u32[]{:S(2)}, u32[]{:S(2)}) collective-permute-start(bf16[768,2048]{1,0:T(8,128)(2,1)} %bitcast.56), channel_id=1, source_target_pairs={{0,16},{16,0},{32,48},{48,32},{64,80},{80,64},{96,112},{112,96},{1... | collective-permute-start | bytes 9437192 | tf_op jit(solution)/shard_map/ppermute | solution.py:469
  78.2 5.3 %collective-permute-start.6 = (bf16[4,16,2048]{2,1,0:T(8,128)(2,1)S(1)}, bf16[4,16,2048]{2,1,0:T(8,128)(2,1)S(1)}, u32[]{:S(2)}, u32[]{:S(2)}) collective-permute-start(bf16[4,16,2048]{2,1,0:T(8,128)(2,1)S(1)} %mix.3.refs_4_), channel_id=1, source_target_pairs={{0,32},{16,48},{32,0},{48,16},{64,96},{80,112},{96,64},{112,80},{1... | collective-permute-start | bytes 786440 | tf_op jit(solution)/shard_map/ppermute | solution.py:509
  146.7 6.8 %collective-permute-start.7 = (bf16[4,16,2048]{2,1,0:T(8,128)(2,1)S(1)}, bf16[4,16,2048]{2,1,0:T(8,128)(2,1)S(1)}, u32[]{:S(2)}, u32[]{:S(2)}) collective-permute-start(bf16[4,16,2048]{2,1,0:T(8,128)(2,1)S(1)} %mix.4.refs_5_), channel_id=1, source_target_pairs={{0,96},{16,112},{32,64},{48,80},{64,32},{80,48},{96,0},{112,16},{1... | collective-permute-start | bytes 786440 | tf_op jit(solution)/shard_map/ppermute | solution.py:509
  218.9 13.5 %collective-permute-start.8 = (bf16[4,16,2048]{2,1,0:T(8,128)(2,1)S(1)}, bf16[4,16,2048]{2,1,0:T(8,128)(2,1)S(1)}, u32[]{:S(2)}, u32[]{:S(2)}) collective-permute-start(bf16[4,16,2048]{2,1,0:T(8,128)(2,1)S(1)} %mix.5.refs_6_), channel_id=1, source_target_pairs={{0,32},{16,48},{32,0},{48,16},{64,96},{80,112},{96,64},{112,80},{1... | collective-permute-start | bytes 786440 | tf_op jit(solution)/shard_map/ppermute | solution.py:509
  304.2 11.6 %collective-permute-start.9 = (bf16[4,16,2048]{2,1,0:T(8,128)(2,1)S(1)}, bf16[4,16,2048]{2,1,0:T(8,128)(2,1)S(1)}, u32[]{:S(2)}, u32[]{:S(2)}) collective-permute-start(bf16[4,16,2048]{2,1,0:T(8,128)(2,1)S(1)} %get-tuple-element.102), channel_id=1, source_target_pairs={{0,16},{16,0},{32,48},{48,32},{64,80},{80,64},{96,112},{112,96},{1... | collective-permute-start | bytes 786440 | tf_op jit(solution)/shard_map/ppermute | solution.py:469
